TPU v7x, 256 devices: a whole 4x4x8 slice. The times are simulated.
256 devices in a mesh: bond: 32 (over x, y, core), mpo: 8 (over z).
Axes of the slice: x: 4, y: 4, z: 8, core: 2. Of those that a mesh axis runs over, the one named last changes fastest.
Arguments:
- wavefunction: bfloat16 [16, 1024, 1024], P(None, 'bond'), may hold values from -6 to 6
- left_env: bfloat16 [24, 32, 512, 1024], P('mpo', 'bond'), may hold values from -0.0390625 to 0.0390625
- right_env: bfloat16 [24, 32, 512, 1024], P('mpo', 'bond'), may hold values from -0.1875 to 0.1875
- left_sizes: int32 [16], replicated, may hold values from 512 to 1024, as said below
- right_sizes: int32 [16], replicated, may hold values from 512 to 1024, as said below
- channel_shift: int32 [24], replicated, may hold values from -1 to 1, as said below
Outputs:
- first_step: bfloat16 [16, 1024, 1024], P(None, 'bond', 'mpo')
- second_step: bfloat16 [16, 1024, 1024], P(None, 'bond', 'mpo')
Inputs may be any that keep to these rules, and one draw needn't show every extreme that they name: `left_sizes`: some sector has exactly 1024 left states. `right_sizes`: some sector has exactly 1024 right states. `channel_shift`: each aligned block of 3 consecutive channels holds -1, 0 and 1 once each.
All inputs are finite; a program needn't handle non-finite values.
Results may differ from a plain program's by a relative error of at most 0.025.
Values may be sent and summed in bfloat16 or wider, within the bound.
A program may use at most 128 MiB of HBM per device.

v0:
```python
import jax
import jax.numpy as jnp
from jax import lax
from jax.experimental import pallas as pl
from jax.experimental.pallas import tpu as pltpu
from jax.sharding import PartitionSpec as P

MESH = pl.DeviceIdType.MESH
PIECES = 2


def kernel(
    wave,
    left_env,
    right_env,
    left_sizes,
    right_sizes,
    channel_shift,
    first_out,
    second_out,
    left,
    right,
    start_in,
    full,
    mixed,
    near,
    moved_out,
    moved_in,
    part_out,
    part_in,
    last,
    local_sem,
    pair_sem,
    scatter_sem,
    ring_send,
    ring_recv,
    cross_send,
    cross_recv,
    moved_send,
    moved_recv,
    part_send,
    part_recv,
    back_send,
    back_recv,
):
    bonds = lax.axis_size("bond")
    groups = lax.axis_size("mpo")
    me = lax.axis_index("bond")
    z = lax.axis_index("mpo")
    sectors = bonds // 2
    q = me // 2
    h = me % 2
    half = wave.shape[1] // 2
    rows = bonds * half
    cols = full.shape[-1]
    per_chunk = right.shape[1] // groups
    lines = bonds // PIECES
    piece_rows = rows // PIECES
    turn = 1 - 2 * h
    partner = (me + turn, z)
    ahead = (me, (z + turn + groups) % groups)
    behind = (me, (z - turn + groups) % groups)
    hops = groups // 2

    def chunk_at(offset):
        return (z + turn * offset + groups) % groups

    def remote(source, target, send, recv, device):
        return pltpu.make_async_remote_copy(
            src_ref=source,
            dst_ref=target,
            send_sem=send,
            recv_sem=recv,
            device_id=device,
            device_id_type=MESH,
        )

    right_own = right.at[:, :, h]
    load_left = pltpu.make_async_copy(left_env, left, local_sem.at[0])
    load_right = pltpu.make_async_copy(right_env, right_own, local_sem.at[1])
    load_left.start()
    load_right.start()

    barrier = pltpu.get_barrier_semaphore()

    def greet(i, carry):
        pl.semaphore_signal(
            barrier, inc=1, device_id=((me + i) % bonds, z), device_id_type=MESH
        )
        return carry

    pl.semaphore_signal(barrier, inc=1, device_id=ahead, device_id_type=MESH)
    pl.semaphore_signal(barrier, inc=1, device_id=behind, device_id_type=MESH)
    lax.fori_loop(1, bonds, greet, 0)
    pl.semaphore_wait(barrier, bonds + 1)

    my_cols = pl.ds(pl.multiple_of(z * cols, cols), cols)

    def piece_of_wave(p):
        return wave.at[p // 2, pl.ds(pl.multiple_of((p % 2) * half, half), half), my_cols]

    def scatter(i, carry):
        p = (me + i) % bonds
        remote(
            piece_of_wave(p), start_in.at[me], scatter_sem.at[0], scatter_sem.at[1], (p, z)
        ).start()
        return carry

    lax.fori_loop(1, bonds, scatter, 0)
    keep = pltpu.make_async_copy(piece_of_wave(me), start_in.at[me], local_sem.at[2])
    keep.start()
    others = start_in.at[pl.ds(0, bonds - 1)]

    @pl.when(q == 0)
    def _():
        for step in range(2):
            moved_in[step, 0] = jnp.zeros(moved_in.shape[2:], moved_in.dtype)

    @pl.when(q == sectors - 1)
    def _():
        for step in range(2):
            moved_in[step, 1] = jnp.zeros(moved_in.shape[2:], moved_in.dtype)

    row = lax.broadcasted_iota(jnp.int32, (rows, cols), 0)
    col = lax.broadcasted_iota(jnp.int32, (rows, cols), 1)
    row = (row // half) * (2 * half) + h * half + row % half
    live = (row < left_sizes[q]) & (col + z * cols < right_sizes[q])

    channels = left.shape[0]

    def channel_of(shift):
        found = channels - 1
        for j in range(channels - 1):
            found = jnp.where(channel_shift[z * channels + j] == shift, j, found)
        return found

    order = [channel_of(1), channel_of(-1), channel_of(0)]

    keep.wait()
    remote(others, others, scatter_sem.at[0], scatter_sem.at[1], partner).wait()
    initial = jnp.where(live, start_in[...].reshape(rows, cols), jnp.zeros((), start_in.dtype))
    full[0, z, :, h] = initial.reshape(bonds, half, cols)

    load_right.wait()
    swap_right = remote(right_own, right_own, pair_sem.at[0], pair_sem.at[1], partner)

    def apply(step, carry):
        def line_set(chunk, piece):
            return full.at[step, chunk, pl.ds(piece * lines, lines), h]

        def pass_on(chunk, slot, piece, device):
            block = line_set(chunk, piece)
            return remote(
                block, block, ring_send.at[step], ring_recv.at[step, slot, piece], device
            )

        def share(chunk, piece):
            block = line_set(chunk, piece)
            return remote(
                block, block, cross_send.at[step], cross_recv.at[step, chunk, piece], partner
            )

        def mix(chunks):
            vector = []
            for chunk in chunks:
                for piece in range(PIECES):
                    share(chunk, piece).wait_recv()
                vector.append(full[step, chunk].reshape(2 * rows, cols))
            vector = vector[0] if len(vector) == 1 else jnp.concatenate(vector, axis=1)
            for d in range(channels):
                block = jnp.dot(
                    left[order[d]], vector, preferred_element_type=jnp.float32
                ).astype(mixed.dtype)
                for n, chunk in enumerate(chunks):
                    mixed[d, :, pl.ds(pl.multiple_of(chunk * cols, cols), cols)] = block[
                        :, n * cols : (n + 1) * cols
                    ]

        for piece in range(PIECES):
            pass_on(z, 0, piece, ahead).start()
            pass_on(z, 1, piece, behind).start()
        for piece in range(PIECES):
            share(z, piece).start()

        @pl.when(step == 0)
        def _():
            swap_right.start()
            load_left.wait()

        @pl.when(step == 1)
        def _():
            send_back(first_out, full.at[1, z, :, h], 0)

        pending = [z]
        for s in range(1, hops + 1):
            from_behind, from_ahead = chunk_at(-s), chunk_at(s)
            now = [from_behind]
            if s < hops:
                now.append(from_ahead)
            for piece in range(PIECES):
                pass_on(from_behind, 2 * s - 2, piece, ahead).wait_recv()
                if s < hops:
                    pass_on(from_behind, 2 * s, piece, ahead).start()
                share(from_behind, piece).start()
                if s < hops:
                    pass_on(from_ahead, 2 * s - 1, piece, behind).wait_recv()
                    if s < hops - 1:
                        pass_on(from_ahead, 2 * s + 1, piece, behind).start()
                    share(from_ahead, piece).start()
            mix(pending)
            pending = now
        mix(pending)

        @pl.when(step == 0)
        def _():
            swap_right.wait()

        def order_of(k):
            distance = hops - (k + 1) // 2
            return chunk_at(distance * (1 - 2 * (k % 2)))

        def image(d, chunk):
            block = right[order[d], pl.ds(chunk * per_chunk, per_chunk)]
            return lax.dot_general(
                mixed[d],
                block.reshape(cols, block.shape[-1]),
                (((1,), (1,)), ((), ())),
                preferred_element_type=jnp.float32,
            )

        def to_sector(d, chunk, k, device=partner):
            return remote(
                moved_out.at[d, chunk],
                moved_in.at[step, d, chunk],
                moved_send.at[d],
                moved_recv.at[step, d, k],
                device,
            )

        has_target = [q < sectors - 1, q > 0]
        has_source = [q > 0, q < sectors - 1]

        def moved_chunk(k, inner):
            chunk = order_of(k)
            for d in range(2):
                moved_out[d, chunk] = image(d, chunk).astype(moved_out.dtype)

                @pl.when(has_target[d])
                def _():
                    to_sector(d, chunk, k, (me + (2 if d == 0 else -2), z)).start()

            return inner

        def near_chunk(k, inner):
            chunk = order_of(k)
            near[chunk] = image(2, chunk)
            return inner

        lax.fori_loop(0, groups, moved_chunk, 0)
        lax.fori_loop(0, groups, near_chunk, 0)

        def partial(k, piece, device):
            part = pl.ds(piece * piece_rows, piece_rows)
            return remote(
                part_out.at[k, part],
                part_in.at[step, k, part],
                part_send.at[0],
                part_recv.at[step, k, piece],
                device,
            )

        def gathered(k, chunk, part):
            return (
                near[chunk, part]
                + moved_in[step, 0, chunk, part].astype(jnp.float32)
                + moved_in[step, 1, chunk, part].astype(jnp.float32)
            )

        def await_moved(k, chunk):
            for d in range(2):

                @pl.when(has_source[d])
                def _():
                    to_sector(d, chunk, k).wait_recv()

        for k in range(groups - 1):
            chunk = order_of(k)
            device = ahead if k % 2 == 0 else behind
            await_moved(k, chunk)
            for piece in range(PIECES):
                part = pl.ds(piece * piece_rows, piece_rows)
                total = gathered(k, chunk, part)
                if k >= 2:
                    partial(k - 2, piece, device).wait_recv()
                    total += part_in[step, k - 2, part].astype(jnp.float32)
                part_out[k, part] = total.astype(part_out.dtype)
                partial(k, piece, device).start()

        await_moved(groups - 1, z)
        total = gathered(groups - 1, z, pl.ds(0, rows))
        for k in (groups - 3, groups - 2):
            for piece in range(PIECES):
                partial(k, piece, ahead).wait_recv()
            total += part_in[step, k].astype(jnp.float32)
        total = jnp.where(live, total, 0.0)

        for d in range(2):

            @pl.when(has_target[d])
            def _():
                remote(
                    moved_out.at[d], moved_out.at[d], moved_send.at[d], moved_send.at[d], partner
                ).wait_send()

        remote(part_out, part_out, part_send.at[0], part_send.at[0], partner).wait_send()
        sent = full.at[step, pl.ds(0, groups - 1), :, 0]
        remote(sent, sent, ring_send.at[step], ring_send.at[step], partner).wait_send()
        sent = full.at[step, :, :, 0]
        remote(sent, sent, cross_send.at[step], cross_send.at[step], partner).wait_send()

        @pl.when(step == 0)
        def _():
            full[1, z, :, h] = total.astype(full.dtype).reshape(bonds, half, cols)

        @pl.when(step == 1)
        def _():
            begin = full[0, z, :, h].reshape(rows, cols).astype(jnp.float32)
            last[...] = (2.0 * total - begin).astype(last.dtype).reshape(bonds, half, cols)

        return carry

    def send_back(out, block, slot):
        def one(i, carry):
            p = (me + i) % bonds
            remote(
                block.at[p], out.at[q, h], back_send.at[slot], back_recv.at[slot], (p, z)
            ).start()
            return carry

        lax.fori_loop(1, bonds, one, 0)
        pltpu.make_async_copy(block.at[me], out.at[q, h], local_sem.at[3 + slot]).start()

    def finish(out, block, slot):
        pltpu.make_async_copy(block.at[me], out.at[q, h], local_sem.at[3 + slot]).wait()
        remote(others, others, back_send.at[slot], back_recv.at[slot], partner).wait()

    lax.fori_loop(0, 2, apply, 0)
    send_back(second_out, last, 1)
    finish(first_out, full.at[1, z, :, h], 0)
    finish(second_out, last, 1)


def local(wavefunction, left_env, right_env, left_sizes, right_sizes, channel_shift):
    bonds = lax.axis_size("bond")
    groups = lax.axis_size("mpo")
    sectors, block_rows, states = wavefunction.shape
    half = block_rows // 2
    channels = left_env.shape[0]
    rows = bonds * half
    cols = states // groups
    out = jax.ShapeDtypeStruct((sectors, 2, half, cols), wavefunction.dtype)
    dtype = wavefunction.dtype
    dma = pltpu.SemaphoreType.DMA
    first, second = pl.pallas_call(
        kernel,
        out_shape=(out, out),
        in_specs=[pl.BlockSpec(memory_space=pl.ANY)] * 3
        + [pl.BlockSpec(memory_space=pltpu.SMEM)] * 3,
        out_specs=[pl.BlockSpec(memory_space=pl.ANY)] * 2,
        scratch_shapes=[
            pltpu.VMEM((channels, rows, states), dtype),
            pltpu.VMEM((channels, bonds, 2, half, states), dtype),
            pltpu.VMEM((bonds, half, cols), dtype),
            pltpu.VMEM((2, groups, bonds, 2, half, cols), dtype),
            pltpu.VMEM((channels, rows, states), dtype),
            pltpu.VMEM((groups, rows, cols), jnp.float32),
            pltpu.VMEM((2, groups, rows, cols), dtype),
            pltpu.VMEM((2, 2, groups, rows, cols), dtype),
            pltpu.VMEM((groups - 1, rows, cols), dtype),
            pltpu.VMEM((2, groups - 1, rows, cols), dtype),
            pltpu.VMEM((bonds, half, cols), dtype),
            dma((5,)),
            dma((2,)),
            dma((2,)),
            dma((2,)),
            dma((2, groups, PIECES)),
            dma((2,)),
            dma((2, groups, PIECES)),
            dma((2,)),
            dma((2, 2, groups)),
            dma((1,)),
            dma((2, groups - 1, PIECES)),
            dma((2,)),
            dma((2,)),
        ],
        compiler_params=pltpu.CompilerParams(
            collective_id=0, has_side_effects=True, vmem_limit_bytes=56 << 20
        ),
        cost_estimate=pl.CostEstimate(
            flops=8 * channels * rows * states * states,
            bytes_accessed=6 * channels * rows * states,
            transcendentals=0,
        ),
        name="two_steps",
    )(
        wavefunction,
        left_env.reshape(channels, rows, states),
        right_env.reshape(channels, bonds, half, states),
        left_sizes,
        right_sizes,
        channel_shift,
    )
    shape = (sectors, block_rows, cols)
    return first.reshape(shape), second.reshape(shape)


def solution(mesh):
    placed = (
        P(None, "bond", None),
        P("mpo", "bond", None, None),
        P("mpo", "bond", None, None),
        P(),
        P(),
        P(),
    )
    return jax.shard_map(
        local,
        mesh=mesh,
        in_specs=placed,
        out_specs=(P(None, "bond", "mpo"), P(None, "bond", "mpo")),
        check_vma=False,
    )
```

profile of v0, /device:TPU:1, one launch (start us, length us, event | category | flops | bytes accessed | tf_op | source)
XLA Modules:
  0.0 127.0 jit_solution(12275314254587135893)
XLA Ops:
  0.6 123.3 %two_steps.1 = (bf16[16,2,16,128]{3,2,1,0:T(8,128)(2,1)}, bf16[16,2,16,128]{3,2,1,0:T(8,128)(2,1)}) custom-call(bf16[16,32,1024]{2,1,0:T(8,128)(2,1)} %wave.1, bf16[3,512,1024]{2,1,0:T(8,128)(2,1)} %bitcast.6, bf16[3,32,16,1024]{3,2,1,0:T(8,128)(2,1)} %bitcast.7, s32[16]{0:T(128)} %left_sizes.1, s32[16]{0:T(128)} %right_sizes.1, s32[24]{0:T(128)} %channel_shift.1), custom_call_target="tpu_custom_call" | custom-call | flops 12884901888 | bytes 9437184 | tf_op jit(solution)/shard_map/two_steps/pallas_call | solution.py:364
  123.9 1.6 %copy.10 = bf16[16,32,128]{2,1,0:T(8,128)(2,1)} copy(bf16[16,32,128]{2,1,0:T(8,128)(2,1)} %bitcast.5) | data formatting | bytes 262144
  125.5 1.6 %copy.11 = bf16[16,32,128]{2,1,0:T(8,128)(2,1)} copy(bf16[16,32,128]{2,1,0:T(8,128)(2,1)} %bitcast.4) | data formatting | bytes 262144
where the time goes:
time: 127 us
  Pallas kernels  123 us (97%)
  local copies, waits for them, and re-layouts  3.14 us (2%)
    pallas_call x1, Pallas kernels, local(): pl.pallas_call(kernel, out_shape=(out, out), in_specs=[pl.BlockSpec(memor...  123 us
    unnamed x2, local copies, waits for them, and re-layouts  3.14 us

commit v1 on v0

v1 whole, which is shorter than its diff:
```python
import jax
import jax.numpy as jnp
from jax import lax
from jax.experimental import pallas as pl
from jax.experimental.pallas import tpu as pltpu
from jax.sharding import PartitionSpec as P

MESH = pl.DeviceIdType.MESH
PIECES = 2
Z_PART = 8
LAG = 1


def z_first_rows(rows):
    return rows * Z_PART // 32


def kernel(
    wave,
    left_env,
    right_env,
    left_sizes,
    right_sizes,
    channel_shift,
    first_out,
    second_out,
    left,
    right,
    start_in,
    full,
    mixed,
    near,
    moved_out,
    moved_in,
    y_part_out,
    y_part_in,
    z_part_out,
    z_part_in,
    late_out,
    late_in,
    last,
    local_sem,
    pair_sem,
    keep_sem,
    scatter_send,
    scatter_recv,
    ring_send,
    ring_recv,
    side_recv,
    cross_send,
    cross_recv,
    moved_send,
    moved_recv,
    part_send,
    y_part_recv,
    z_part_recv,
    late_send,
    late_recv,
    back_send,
    back_recv,
):
    bonds = lax.axis_size("bond")
    groups = lax.axis_size("mpo")
    me = lax.axis_index("bond")
    z = lax.axis_index("mpo")
    sectors = bonds // 2
    q = me // 2
    h = me % 2
    channels = left.shape[0]
    half = wave.shape[1] // 2
    rows = bonds * half
    cols = full.shape[-1]
    per_chunk = right.shape[1] // groups
    lines = bonds // PIECES
    y_rows = moved_in.shape[3]
    z_rows = rows - y_rows
    y_span = pl.ds(0, y_rows)
    z_span = pl.ds(y_rows, z_rows)
    turn = 1 - 2 * h
    partner = (me + turn, z)
    hops = groups // 2

    def chunk_at(offset):
        return (z + turn * offset + groups) % groups

    ahead = (me, chunk_at(1))
    behind = (me, chunk_at(-1))

    def remote(source, target, send, recv, device):
        return pltpu.make_async_remote_copy(
            src_ref=source,
            dst_ref=target,
            send_sem=send,
            recv_sem=recv,
            device_id=device,
            device_id_type=MESH,
        )

    def await_sent(block, sem):
        remote(block, block, sem, sem, partner).wait_send()

    right_own = right.at[:, :, h]
    load_left = pltpu.make_async_copy(left_env, left, local_sem.at[0])
    load_right = pltpu.make_async_copy(right_env, right_own, local_sem.at[1])
    swap_right = remote(right_env, right_own, pair_sem.at[0], pair_sem.at[1], partner)
    load_left.start()
    load_right.start()

    barrier = pltpu.get_barrier_semaphore()

    def greet(i, carry):
        pl.semaphore_signal(
            barrier, inc=1, device_id=((me + i) % bonds, z), device_id_type=MESH
        )
        return carry

    pl.semaphore_signal(barrier, inc=1, device_id=ahead, device_id_type=MESH)
    pl.semaphore_signal(barrier, inc=1, device_id=behind, device_id_type=MESH)
    lax.fori_loop(1, bonds, greet, 0)
    pl.semaphore_wait(barrier, bonds + 1)

    swap_right.start()

    def piece_of_wave(p, chunk):
        return wave.at[
            p // 2,
            pl.ds(pl.multiple_of((p % 2) * half, half), half),
            pl.ds(pl.multiple_of(chunk * cols, cols), cols),
        ]

    ours = [z % 2 + 2 * j for j in range(hops)]
    theirs = [1 - z % 2 + 2 * j for j in range(hops)]

    def scatter(j, i):
        p = (me + i) % bonds
        remote(
            piece_of_wave(p, ours[j]),
            start_in.at[j, me],
            scatter_send.at[0],
            scatter_recv.at[j],
            (p, z),
        ).start()

    def keep(j):
        return pltpu.make_async_copy(piece_of_wave(me, ours[j]), start_in.at[j, me], keep_sem.at[j])

    for j in range(hops):

        def spread(i, carry, j=j):
            scatter(j, i)
            return carry

        keep(j).start()
        lax.fori_loop(1, bonds, spread, 0)

    for step in range(2):
        for d, outside in ((0, 0), (1, sectors - 1)):

            @pl.when(q == outside)
            def _():
                moved_in[step, d] = jnp.zeros(moved_in.shape[2:], moved_in.dtype)
                late_in[step, d] = jnp.zeros(late_in.shape[2:], late_in.dtype)

        for k in range(2):
            y_part_in[step, k] = jnp.zeros(y_part_in.shape[2:], y_part_in.dtype)
            z_part_in[step, k] = jnp.zeros(z_part_in.shape[2:], z_part_in.dtype)

    def live(first, count, chunk=z):
        row = lax.broadcasted_iota(jnp.int32, (count, cols), 0) + first
        col = lax.broadcasted_iota(jnp.int32, (count, cols), 1)
        row = (row // half) * (2 * half) + h * half + row % half
        return (row < left_sizes[q]) & (col + chunk * cols < right_sizes[q])

    def channel_of(shift):
        found = channels - 1
        for j in range(channels - 1):
            found = jnp.where(channel_shift[z * channels + j] == shift, j, found)
        return found

    order = [channel_of(1), channel_of(-1), channel_of(0)]

    def apply(step, carry):
        def line_set(chunk, piece):
            return full.at[step, chunk, pl.ds(piece * lines, lines), h]

        def pass_on(chunk, slot, piece, device):
            block = line_set(chunk, piece)
            return remote(block, block, ring_send.at[0], ring_recv.at[slot, piece], device)

        def share(chunk, piece):
            block = line_set(chunk, piece)
            return remote(
                block, block, cross_send.at[0], cross_recv.at[step, chunk, piece], partner
            )

        def mix_units(chunks):
            def unit(d):
                if d == 0:
                    for chunk in chunks:
                        for piece in range(PIECES):
                            share(chunk, piece).wait_recv()
                sets = [chunks]
                for some in sets:
                    vector = [full[step, chunk].reshape(2 * rows, cols) for chunk in some]
                    vector = vector[0] if len(vector) == 1 else jnp.concatenate(vector, axis=1)
                    block = jnp.dot(
                        left[order[d]], vector, preferred_element_type=jnp.float32
                    ).astype(mixed.dtype)
                    for n, chunk in enumerate(some):
                        mixed[d, :, pl.ds(pl.multiple_of(chunk * cols, cols), cols)] = block[
                            :, n * cols : (n + 1) * cols
                        ]

            return [lambda d=d: unit(d) for d in range(channels)]

        def run(queue, count=channels):
            for unit in queue[:count]:
                unit()
            del queue[:count]

        def to_side(j, chunk, way):
            block = full.at[0, chunk, :, h]
            return remote(
                block, block, ring_send.at[0], side_recv.at[j], (me, (z + way + groups) % groups)
            )

        @pl.when(step == 0)
        def _():
            def begin(j):
                keep(j).wait()
                others = start_in.at[j, pl.ds(0, bonds - 1)]
                remote(others, others, scatter_send.at[0], scatter_recv.at[j], partner).wait_recv()
                block = start_in[j].reshape(rows, cols)
                block = jnp.where(live(0, rows, ours[j]), block, jnp.zeros((), block.dtype))
                full[0, ours[j], :, h] = block.reshape(bonds, half, cols)
                to_side(j, ours[j], 1 - 2 * (j % 2)).start()
                for piece in range(PIECES):
                    share(ours[j], piece).start()

            def arrive(j):
                to_side(j, theirs[j], 1).wait_recv()
                for piece in range(PIECES):
                    share(theirs[j], piece).start()

            begin(0)
            begin(1)
            load_left.wait()
            queue = mix_units(ours[:2])
            for j in range(2, hops):
                begin(j)
                run(queue, 1)
            run(queue)
            queue = mix_units(ours[2:]) if hops > 2 else []
            for j in range(hops):
                arrive(j)
                run(queue, 1 + j % 2)
                if j % 2:
                    queue += mix_units(theirs[j - 1 : j + 1])
            run(queue, len(queue))
            sent = start_in.at[:, pl.ds(0, bonds - 1)]
            await_sent(sent, scatter_send.at[0])
            await_sent(full.at[0, pl.ds(0, hops), :, 0], ring_send.at[0])
            load_right.wait()
            swap_right.wait()

        @pl.when(step == 1)
        def _():
            for piece in range(PIECES):
                pass_on(z, 0, piece, ahead).start()
                pass_on(z, 1, piece, behind).start()
            for piece in range(PIECES):
                share(z, piece).start()
            send_back(first_out, full.at[1, z, :, h], 0)
            queue = mix_units([z])
            run(queue)
            for s in range(1, hops + 1):
                from_behind, from_ahead = chunk_at(-s), chunk_at(s)
                for piece in range(PIECES):
                    pass_on(from_behind, 2 * s - 2, piece, ahead).wait_recv()
                    if s < hops:
                        pass_on(from_behind, 2 * s, piece, ahead).start()
                    share(from_behind, piece).start()
                    if s < hops:
                        pass_on(from_ahead, 2 * s - 1, piece, behind).wait_recv()
                        if s < hops - 1:
                            pass_on(from_ahead, 2 * s + 1, piece, behind).start()
                        share(from_ahead, piece).start()
                    run(queue, 2 - piece)
                run(queue)
                queue = mix_units([from_behind, from_ahead] if s < hops else [from_behind])
            run(queue)
            await_sent(full.at[1, pl.ds(0, groups - 1), :, 0], ring_send.at[0])

        def order_of(k):
            distance = hops - (k + 1) // 2
            return chunk_at(distance * (1 - 2 * (k % 2)))

        def images(d, pair):
            blocks = [
                right[order[d], pl.ds(chunk * per_chunk, per_chunk)].reshape(cols, -1)
                for chunk in pair
            ]
            both = lax.dot_general(
                mixed[d],
                jnp.concatenate(blocks, axis=0),
                (((1,), (1,)), ((), ())),
                preferred_element_type=jnp.float32,
            )
            return both[:, :cols], both[:, cols:]

        has_target = [(q < sectors - 1), (q > 0)]
        has_source = [(q > 0), (q < sectors - 1)]

        def to_sector(d, chunk, k, device=partner):
            return remote(
                moved_out.at[d, chunk, y_span],
                moved_in.at[step, d, chunk],
                moved_send.at[d],
                moved_recv.at[step, d, k],
                device,
            )

        def late(d, device=partner):
            return remote(
                late_out.at[d], late_in.at[step, d], late_send.at[d], late_recv.at[step, d], device
            )

        def neighbour(d):
            return (me + (2 if d == 0 else -2), z)

        def way_of(k):
            return (me, chunk_at(1 - 2 * (k % 2)))

        def z_partial(k, device=partner):
            return remote(
                z_part_out.at[k],
                z_part_in.at[step, k + 2],
                part_send.at[0],
                z_part_recv.at[step, k],
                device,
            )

        def y_part(piece):
            return pl.ds(piece * (y_rows // PIECES), y_rows // PIECES)

        def y_partial(k, piece, device=partner):
            return remote(
                y_part_out.at[k, y_part(piece)],
                y_part_in.at[step, k + 2, y_part(piece)],
                part_send.at[1],
                y_part_recv.at[step, k, piece],
                device,
            )

        def z_terms(chunk):
            return [
                near[chunk, z_span],
                moved_out[0, chunk, z_span].astype(jnp.float32),
                moved_out[1, chunk, z_span].astype(jnp.float32),
            ]

        def y_terms(chunk, part=y_span):
            return (
                near[chunk, part]
                + moved_in[step, 0, chunk, part].astype(jnp.float32)
                + moved_in[step, 1, chunk, part].astype(jnp.float32)
            )

        def await_moved(k, chunk):
            for d in range(2):

                @pl.when(has_source[d])
                def _():
                    to_sector(d, chunk, k).wait_recv()

        def z_hop(k):
            chunk = order_of(k)

            @pl.when((k >= 2))
            def _():
                z_partial(k - 2).wait_recv()

            for i, term in enumerate(z_terms(chunk)):
                term += z_part_in[step, k, i].astype(jnp.float32)
                z_part_out[k, i] = term.astype(z_part_out.dtype)
            z_partial(k, way_of(k)).start()

        def y_hop(k):
            chunk = order_of(k)
            await_moved(k, chunk)
            for piece in range(PIECES):
                part = y_part(piece)

                @pl.when((k >= 2))
                def _():
                    y_partial(k - 2, piece).wait_recv()

                total = y_terms(chunk, part) + y_part_in[step, k, part].astype(jnp.float32)
                y_part_out[k, part] = total.astype(y_part_out.dtype)
                y_partial(k, piece, way_of(k)).start()

        def round_of_ring(t, inner):
            @pl.when(t < hops)
            def _():
                pair = (order_of(2 * t), order_of(2 * t + 1))
                for d in range(2):
                    blocks = images(d, pair)
                    for n, chunk in enumerate(pair):
                        moved_out[d, chunk] = blocks[n].astype(moved_out.dtype)

                        @pl.when(has_target[d])
                        def _():
                            to_sector(d, chunk, 2 * t + n, neighbour(d)).start()

                near[pair[0]], near[pair[1]] = images(2, pair)

            for hop, lag in ((z_hop, 1), (y_hop, LAG)):

                @pl.when((t >= lag) & (t < lag + hops))
                def _():
                    hop(2 * (t - lag))

                @pl.when((t >= lag) & (t < lag + hops - 1))
                def _():
                    hop(2 * (t - lag) + 1)

            return inner

        lax.fori_loop(0, hops + LAG, round_of_ring, 0)

        z_total = z_terms(z)
        for k in (groups - 3, groups - 2):
            z_partial(k).wait_recv()
            for i in range(3):
                z_total[i] += z_part_in[step, k + 2, i].astype(jnp.float32)
        for d in range(2):
            late_out[d] = z_total[1 + d].astype(late_out.dtype)

            @pl.when(has_target[d])
            def _():
                late(d, neighbour(d)).start()

        await_moved(groups - 1, z)
        total = y_terms(z)
        for k in (groups - 3, groups - 2):
            for piece in range(PIECES):
                y_partial(k, piece).wait_recv()
            total += y_part_in[step, k + 2].astype(jnp.float32)

        def conclude(value, first, count):
            value = jnp.where(live(first, count), value, 0.0)
            span = pl.ds(first // half, count // half)
            shape = (count // half, half, cols)

            @pl.when(step == 0)
            def _():
                full[1, z, span, h] = value.astype(full.dtype).reshape(shape)

            @pl.when(step == 1)
            def _():
                begin = full[0, z, span, h].reshape(count, cols).astype(jnp.float32)
                last[span] = (2.0 * value - begin).astype(last.dtype).reshape(shape)

        conclude(total, 0, y_rows)
        for d in range(2):

            @pl.when(has_source[d])
            def _():
                late(d).wait_recv()

        total = (
            z_total[0]
            + late_in[step, 0].astype(jnp.float32)
            + late_in[step, 1].astype(jnp.float32)
        )
        conclude(total, y_rows, z_rows)

        for d in range(2):

            @pl.when(has_target[d])
            def _():
                await_sent(moved_out.at[d, :, y_span], moved_send.at[d])
                late(d).wait_send()

        await_sent(z_part_out, part_send.at[0])
        await_sent(y_part_out, part_send.at[1])
        await_sent(full.at[step, :, :, 0], cross_send.at[0])
        return carry

    def send_back(out, block, slot):
        def one(i, carry):
            p = (me + i) % bonds
            remote(
                block.at[p], out.at[q, h], back_send.at[slot], back_recv.at[slot], (p, z)
            ).start()
            return carry

        lax.fori_loop(1, bonds, one, 0)
        pltpu.make_async_copy(block.at[me], out.at[q, h], local_sem.at[2 + slot]).start()

    def finish(out, block, slot):
        pltpu.make_async_copy(block.at[me], out.at[q, h], local_sem.at[2 + slot]).wait()
        others = start_in.at[0, pl.ds(0, bonds - 1)]
        remote(others, others, back_send.at[slot], back_recv.at[slot], partner).wait()

    lax.fori_loop(0, 2, apply, 0)
    send_back(second_out, last, 1)
    finish(first_out, full.at[1, z, :, h], 0)
    finish(second_out, last, 1)


def local(wavefunction, left_env, right_env, left_sizes, right_sizes, channel_shift):
    bonds = lax.axis_size("bond")
    groups = lax.axis_size("mpo")
    sectors, block_rows, states = wavefunction.shape
    half = block_rows // 2
    channels = left_env.shape[0]
    rows = bonds * half
    cols = states // groups
    z_rows = z_first_rows(rows)
    y_rows = rows - z_rows
    dtype = wavefunction.dtype
    out = jax.ShapeDtypeStruct((sectors, 2, half, cols), dtype)
    dma = pltpu.SemaphoreType.DMA
    first, second = pl.pallas_call(
        kernel,
        out_shape=(out, out),
        in_specs=[pl.BlockSpec(memory_space=pl.ANY)] * 3
        + [pl.BlockSpec(memory_space=pltpu.SMEM)] * 3,
        out_specs=[pl.BlockSpec(memory_space=pl.ANY)] * 2,
        scratch_shapes=[
            pltpu.VMEM((channels, rows, states), dtype),
            pltpu.VMEM((channels, bonds, 2, half, states), dtype),
            pltpu.VMEM((groups // 2, bonds, half, cols), dtype),
            pltpu.VMEM((2, groups, bonds, 2, half, cols), dtype),
            pltpu.VMEM((channels, rows, states), dtype),
            pltpu.VMEM((groups, rows, cols), jnp.float32),
            pltpu.VMEM((2, groups, rows, cols), dtype),
            pltpu.VMEM((2, 2, groups, y_rows, cols), dtype),
            pltpu.VMEM((groups - 1, y_rows, cols), dtype),
            pltpu.VMEM((2, groups + 1, y_rows, cols), dtype),
            pltpu.VMEM((groups - 1, 3, z_rows, cols), dtype),
            pltpu.VMEM((2, groups + 1, 3, z_rows, cols), dtype),
            pltpu.VMEM((2, z_rows, cols), dtype),
            pltpu.VMEM((2, 2, z_rows, cols), dtype),
            pltpu.VMEM((bonds, half, cols), dtype),
            dma((4,)),
            dma((2,)),
            dma((groups // 2,)),
            dma((1,)),
            dma((groups // 2,)),
            dma((1,)),
            dma((groups - 1, PIECES)),
            dma((groups // 2,)),
            dma((1,)),
            dma((2, groups, PIECES)),
            dma((2,)),
            dma((2, 2, groups)),
            dma((2,)),
            dma((2, groups - 1, PIECES)),
            dma((2, groups - 1)),
            dma((2,)),
            dma((2, 2)),
            dma((2,)),
            dma((2,)),
        ],
        compiler_params=pltpu.CompilerParams(
            collective_id=0, has_side_effects=True, vmem_limit_bytes=56 << 20
        ),
        cost_estimate=pl.CostEstimate(
            flops=8 * channels * rows * states * states,
            bytes_accessed=6 * channels * rows * states,
            transcendentals=0,
        ),
        name="two_steps",
    )(
        wavefunction,
        left_env.reshape(channels, rows, states),
        right_env.reshape(channels, bonds, half, states),
        left_sizes,
        right_sizes,
        channel_shift,
    )
    shape = (sectors, block_rows, cols)
    return first.reshape(shape), second.reshape(shape)


def solution(mesh):
    placed = (
        P(None, "bond", None),
        P("mpo", "bond", None, None),
        P("mpo", "bond", None, None),
        P(),
        P(),
        P(),
    )
    return jax.shard_map(
        local,
        mesh=mesh,
        in_specs=placed,
        out_specs=(P(None, "bond", "mpo"), P(None, "bond", "mpo")),
        check_vma=False,
    )
```

time: 127 us -> 111 us (0.87)
  Pallas kernels: 123 us -> 107 us
    pallas_call x1, Pallas kernels: 123 us -> 107 us  [local(): pl.pallas_call(kernel, out_shape=(out, out), in_specs=[pl.BlockSpec(memor...]
where the time goes in v1:
time: 111 us
  Pallas kernels  107 us (96%)
  local copies, waits for them, and re-layouts  3.14 us (3%)
    pallas_call x1, Pallas kernels, local(): pl.pallas_call(kernel, out_shape=(out, out), in_specs=[pl.BlockSpec(memor...  107 us
    unnamed x2, local copies, waits for them, and re-layouts  3.14 us

profile of v1, /device:TPU:1, one launch (start us, length us, event | category | flops | bytes accessed | tf_op | source)
XLA Modules:
  0.0 111.1 jit_solution(4924903087589552802)
XLA Ops:
  0.6 107.3 %two_steps.1 = (bf16[16,2,16,128]{3,2,1,0:T(8,128)(2,1)}, bf16[16,2,16,128]{3,2,1,0:T(8,128)(2,1)}) custom-call(bf16[16,32,1024]{2,1,0:T(8,128)(2,1)} %wave.1, bf16[3,512,1024]{2,1,0:T(8,128)(2,1)} %bitcast.6, bf16[3,32,16,1024]{3,2,1,0:T(8,128)(2,1)} %bitcast.7, s32[16]{0:T(128)} %left_sizes.1, s32[16]{0:T(128)} %right_sizes.1, s32[24]{0:T(128)} %channel_shift.1), custom_call_target="tpu_custom_call" | custom-call | flops 12884901888 | bytes 9437184 | tf_op jit(solution)/shard_map/two_steps/pallas_call | solution.py:525
  107.9 1.6 %copy.10 = bf16[16,32,128]{2,1,0:T(8,128)(2,1)} copy(bf16[16,32,128]{2,1,0:T(8,128)(2,1)} %bitcast.5) | data formatting | bytes 262144
  109.5 1.6 %copy.11 = bf16[16,32,128]{2,1,0:T(8,128)(2,1)} copy(bf16[16,32,128]{2,1,0:T(8,128)(2,1)} %bitcast.4) | data formatting | bytes 262144

commit v2 on v1

--- a/solution.py
+++ b/solution.py
@@ -7,12 +7,7 @@
 
 MESH = pl.DeviceIdType.MESH
 PIECES = 2
-Z_PART = 8
-LAG = 1
-
-
-def z_first_rows(rows):
-    return rows * Z_PART // 32
+REACH = 2
 
 
 def kernel(
@@ -32,10 +27,10 @@
     near,
     moved_out,
     moved_in,
-    y_part_out,
-    y_part_in,
-    z_part_out,
-    z_part_in,
+    part_out,
+    part_in,
+    near_out,
+    beside_in,
     late_out,
     late_in,
     last,
@@ -52,8 +47,9 @@
     moved_send,
     moved_recv,
     part_send,
-    y_part_recv,
-    z_part_recv,
+    part_recv,
+    beside_send,
+    beside_recv,
     late_send,
     late_recv,
     back_send,
@@ -72,10 +68,6 @@
     cols = full.shape[-1]
     per_chunk = right.shape[1] // groups
     lines = bonds // PIECES
-    y_rows = moved_in.shape[3]
-    z_rows = rows - y_rows
-    y_span = pl.ds(0, y_rows)
-    z_span = pl.ds(y_rows, z_rows)
     turn = 1 - 2 * h
     partner = (me + turn, z)
     hops = groups // 2
@@ -85,6 +77,19 @@
 
     ahead = (me, chunk_at(1))
     behind = (me, chunk_at(-1))
+
+    def parent(o):
+        return 0 if abs(o) <= REACH else (REACH if o > 0 else -REACH)
+
+    offsets = range(1 - hops, hops + 1)
+
+    def children(o):
+        return [c for c in offsets if abs(c) > 1 and parent(c) == o]
+
+    far = [o for o in offsets if abs(o) > 1]
+    pairs = [(hops, hops - 1), (1, -1), (1 - hops, 2), (-2, 0)]
+    if hops == 2:
+        pairs = [(2, 1), (-1, 0)]
 
     def remote(source, target, send, recv, device):
         return pltpu.make_async_remote_copy(
@@ -114,10 +119,13 @@
         )
         return carry
 
-    pl.semaphore_signal(barrier, inc=1, device_id=ahead, device_id_type=MESH)
-    pl.semaphore_signal(barrier, inc=1, device_id=behind, device_id_type=MESH)
+    for distance in range(1, REACH + 1):
+        for way in (distance, -distance):
+            pl.semaphore_signal(
+                barrier, inc=1, device_id=(me, chunk_at(way)), device_id_type=MESH
+            )
     lax.fori_loop(1, bonds, greet, 0)
-    pl.semaphore_wait(barrier, bonds + 1)
+    pl.semaphore_wait(barrier, bonds - 1 + 2 * REACH)
 
     swap_right.start()
 
@@ -160,10 +168,6 @@
             def _():
                 moved_in[step, d] = jnp.zeros(moved_in.shape[2:], moved_in.dtype)
                 late_in[step, d] = jnp.zeros(late_in.shape[2:], late_in.dtype)
-
-        for k in range(2):
-            y_part_in[step, k] = jnp.zeros(y_part_in.shape[2:], y_part_in.dtype)
-            z_part_in[step, k] = jnp.zeros(z_part_in.shape[2:], z_part_in.dtype)
 
     def live(first, count, chunk=z):
         row = lax.broadcasted_iota(jnp.int32, (count, cols), 0) + first
@@ -270,7 +274,6 @@
                 pass_on(z, 1, piece, behind).start()
             for piece in range(PIECES):
                 share(z, piece).start()
-            send_back(first_out, full.at[1, z, :, h], 0)
             queue = mix_units([z])
             run(queue)
             for s in range(1, hops + 1):
@@ -291,10 +294,6 @@
             run(queue)
             await_sent(full.at[1, pl.ds(0, groups - 1), :, 0], ring_send.at[0])
 
-        def order_of(k):
-            distance = hops - (k + 1) // 2
-            return chunk_at(distance * (1 - 2 * (k % 2)))
-
         def images(d, pair):
             blocks = [
                 right[order[d], pl.ds(chunk * per_chunk, per_chunk)].reshape(cols, -1)
@@ -311,12 +310,13 @@
         has_target = [(q < sectors - 1), (q > 0)]
         has_source = [(q > 0), (q < sectors - 1)]
 
-        def to_sector(d, chunk, k, device=partner):
+        def to_sector(d, o, device=partner):
+            chunk = chunk_at(o)
             return remote(
-                moved_out.at[d, chunk, y_span],
+                moved_out.at[d, chunk],
                 moved_in.at[step, d, chunk],
-                moved_send.at[d],
-                moved_recv.at[step, d, k],
+                moved_send.at[d, o + hops - 1],
+                moved_recv.at[step, d, o + hops - 1],
                 device,
             )
 
@@ -328,124 +328,139 @@
         def neighbour(d):
             return (me + (2 if d == 0 else -2), z)
 
-        def way_of(k):
-            return (me, chunk_at(1 - 2 * (k % 2)))
-
-        def z_partial(k, device=partner):
+        def to_beside(o, i):
+            side = (1 - o) // 2
+            source = moved_out.at[i, chunk_at(o)] if i < 2 else near_out.at[side]
             return remote(
-                z_part_out.at[k],
-                z_part_in.at[step, k + 2],
+                source,
+                beside_in.at[step, side, i],
+                beside_send.at[i // 2],
+                beside_recv.at[step, side, i],
+                (me, chunk_at(o)),
+            )
+
+        def partial(o):
+            slot = o + hops - 1
+            return remote(
+                part_out.at[slot],
+                part_in.at[step, slot],
                 part_send.at[0],
-                z_part_recv.at[step, k],
-                device,
-            )
-
-        def y_part(piece):
-            return pl.ds(piece * (y_rows // PIECES), y_rows // PIECES)
-
-        def y_partial(k, piece, device=partner):
-            return remote(
-                y_part_out.at[k, y_part(piece)],
-                y_part_in.at[step, k + 2, y_part(piece)],
-                part_send.at[1],
-                y_part_recv.at[step, k, piece],
-                device,
-            )
-
-        def z_terms(chunk):
-            return [
-                near[chunk, z_span],
-                moved_out[0, chunk, z_span].astype(jnp.float32),
-                moved_out[1, chunk, z_span].astype(jnp.float32),
-            ]
-
-        def y_terms(chunk, part=y_span):
-            return (
-                near[chunk, part]
-                + moved_in[step, 0, chunk, part].astype(jnp.float32)
-                + moved_in[step, 1, chunk, part].astype(jnp.float32)
-            )
-
-        def await_moved(k, chunk):
+                part_recv.at[step, slot],
+                (me, chunk_at(o - parent(o))),
+            )
+
+        def add_children(o, total):
+            for c in children(o):
+                partial(c).wait_recv()
+                total += part_in[step, c + hops - 1].astype(jnp.float32)
+            return total
+
+        def hop(o):
+            chunk = chunk_at(o)
+            total = near[chunk]
             for d in range(2):
 
                 @pl.when(has_source[d])
                 def _():
-                    to_sector(d, chunk, k).wait_recv()
-
-        def z_hop(k):
-            chunk = order_of(k)
-
-            @pl.when((k >= 2))
+                    to_sector(d, o).wait_recv()
+
+                total += moved_in[step, d, chunk].astype(jnp.float32)
+            part_out[o + hops - 1] = add_children(o, total).astype(part_out.dtype)
+            partial(o).start()
+
+        def image_pair(u, inner):
+            first, second = pairs[-1]
+            for t in range(len(pairs) - 1):
+                first = jnp.where(u == t, pairs[t][0], first)
+                second = jnp.where(u == t, pairs[t][1], second)
+            pair = (chunk_at(first), chunk_at(second))
+            for d in range(2):
+                blocks = images(d, pair)
+                for n, chunk in enumerate(pair):
+                    moved_out[d, chunk] = blocks[n].astype(moved_out.dtype)
+                for t, some in enumerate(pairs):
+                    for o in some:
+
+                        if o > REACH or hops == 2 and o == 2:
+
+                            @pl.when((u == t) & has_target[d])
+                            def _():
+                                to_sector(d, o, neighbour(d)).start()
+
+                        if abs(o) == 1:
+
+                            @pl.when((u == t))
+                            def _():
+                                to_beside(o, d).start()
+
+            near[pair[0]], near[pair[1]] = images(2, pair)
+            return inner
+
+        lax.fori_loop(0, len(pairs), image_pair, 0)
+
+        @pl.when(step == 1)
+        def _():
+            send_back(first_out, full.at[1, z, :, h], 0)
+
+        def send_after(o, done):
+            for d in range(2):
+
+                @pl.when(has_target[d])
+                def _():
+                    to_sector(d, done).wait_send()
+                    if o:
+                        to_sector(d, o, neighbour(d)).start()
+                    else:
+                        late(d, neighbour(d)).start()
+
+        def merge_own():
+            for d in range(2):
+                moved = moved_out[d, z].astype(jnp.float32)
+                for o in (1, -1):
+                    to_beside(o, d).wait_recv()
+                    moved += beside_in[step, (1 - o) // 2, d].astype(jnp.float32)
+                late_out[d] = moved.astype(late_out.dtype)
+
+        def send_beside():
+            for o in (1, -1):
+                near_out[(1 - o) // 2] = near[chunk_at(o)].astype(near_out.dtype)
+                to_beside(o, 2).start()
+
+        if hops == 2:
+            send_beside()
+            merge_own()
+            send_after(0, 2)
+            hop(2)
+        else:
+            send_after(-3, 4)
+            hop(4)
+            send_after(2, 3)
+            hop(3)
+            send_beside()
+            send_after(-2, -3)
+            hop(-3)
+            merge_own()
+            send_after(0, 2)
+            hop(2)
+            hop(-2)
+            for d in range(2):
+
+                @pl.when(has_target[d])
+                def _():
+                    to_sector(d, -2).wait_send()
+
+        total = near[z]
+        for o in (1, -1):
+            to_beside(o, 2).wait_recv()
+            total += beside_in[step, (1 - o) // 2, 2].astype(jnp.float32)
+        total = add_children(0, total)
+        for d in range(2):
+
+            @pl.when(has_source[d])
             def _():
-                z_partial(k - 2).wait_recv()
-
-            for i, term in enumerate(z_terms(chunk)):
-                term += z_part_in[step, k, i].astype(jnp.float32)
-                z_part_out[k, i] = term.astype(z_part_out.dtype)
-            z_partial(k, way_of(k)).start()
-
-        def y_hop(k):
-            chunk = order_of(k)
-            await_moved(k, chunk)
-            for piece in range(PIECES):
-                part = y_part(piece)
-
-                @pl.when((k >= 2))
-                def _():
-                    y_partial(k - 2, piece).wait_recv()
-
-                total = y_terms(chunk, part) + y_part_in[step, k, part].astype(jnp.float32)
-                y_part_out[k, part] = total.astype(y_part_out.dtype)
-                y_partial(k, piece, way_of(k)).start()
-
-        def round_of_ring(t, inner):
-            @pl.when(t < hops)
-            def _():
-                pair = (order_of(2 * t), order_of(2 * t + 1))
-                for d in range(2):
-                    blocks = images(d, pair)
-                    for n, chunk in enumerate(pair):
-                        moved_out[d, chunk] = blocks[n].astype(moved_out.dtype)
-
-                        @pl.when(has_target[d])
-                        def _():
-                            to_sector(d, chunk, 2 * t + n, neighbour(d)).start()
-
-                near[pair[0]], near[pair[1]] = images(2, pair)
-
-            for hop, lag in ((z_hop, 1), (y_hop, LAG)):
-
-                @pl.when((t >= lag) & (t < lag + hops))
-                def _():
-                    hop(2 * (t - lag))
-
-                @pl.when((t >= lag) & (t < lag + hops - 1))
-                def _():
-                    hop(2 * (t - lag) + 1)
-
-            return inner
-
-        lax.fori_loop(0, hops + LAG, round_of_ring, 0)
-
-        z_total = z_terms(z)
-        for k in (groups - 3, groups - 2):
-            z_partial(k).wait_recv()
-            for i in range(3):
-                z_total[i] += z_part_in[step, k + 2, i].astype(jnp.float32)
-        for d in range(2):
-            late_out[d] = z_total[1 + d].astype(late_out.dtype)
-
-            @pl.when(has_target[d])
-            def _():
-                late(d, neighbour(d)).start()
-
-        await_moved(groups - 1, z)
-        total = y_terms(z)
-        for k in (groups - 3, groups - 2):
-            for piece in range(PIECES):
-                y_partial(k, piece).wait_recv()
-            total += y_part_in[step, k + 2].astype(jnp.float32)
+                late(d).wait_recv()
+
+            total += late_in[step, d].astype(jnp.float32)
 
         def conclude(value, first, count):
             value = jnp.where(live(first, count), value, 0.0)
@@ -461,29 +476,17 @@
                 begin = full[0, z, span, h].reshape(count, cols).astype(jnp.float32)
                 last[span] = (2.0 * value - begin).astype(last.dtype).reshape(shape)
 
-        conclude(total, 0, y_rows)
-        for d in range(2):
-
-            @pl.when(has_source[d])
-            def _():
-                late(d).wait_recv()
-
-        total = (
-            z_total[0]
-            + late_in[step, 0].astype(jnp.float32)
-            + late_in[step, 1].astype(jnp.float32)
-        )
-        conclude(total, y_rows, z_rows)
+        conclude(total, 0, rows)
 
         for d in range(2):
 
             @pl.when(has_target[d])
             def _():
-                await_sent(moved_out.at[d, :, y_span], moved_send.at[d])
                 late(d).wait_send()
 
-        await_sent(z_part_out, part_send.at[0])
-        await_sent(y_part_out, part_send.at[1])
+        await_sent(moved_out.at[0, pl.ds(0, 4)], beside_send.at[0])
+        await_sent(near_out, beside_send.at[1])
+        await_sent(part_out.at[pl.ds(0, len(far))], part_send.at[0])
         await_sent(full.at[step, :, :, 0], cross_send.at[0])
         return carry
 
@@ -507,6 +510,11 @@
     send_back(second_out, last, 1)
     finish(first_out, full.at[1, z, :, h], 0)
     finish(second_out, last, 1)
+
+
+def hand_over(first, second, first_out, second_out):
+    first_out[...] = first[...]
+    second_out[...] = second[...]
 
 
 def local(wavefunction, left_env, right_env, left_sizes, right_sizes, channel_shift):
@@ -517,8 +525,6 @@
     channels = left_env.shape[0]
     rows = bonds * half
     cols = states // groups
-    z_rows = z_first_rows(rows)
-    y_rows = rows - z_rows
     dtype = wavefunction.dtype
     out = jax.ShapeDtypeStruct((sectors, 2, half, cols), dtype)
     dma = pltpu.SemaphoreType.DMA
@@ -536,13 +542,13 @@
             pltpu.VMEM((channels, rows, states), dtype),
             pltpu.VMEM((groups, rows, cols), jnp.float32),
             pltpu.VMEM((2, groups, rows, cols), dtype),
-            pltpu.VMEM((2, 2, groups, y_rows, cols), dtype),
-            pltpu.VMEM((groups - 1, y_rows, cols), dtype),
-            pltpu.VMEM((2, groups + 1, y_rows, cols), dtype),
-            pltpu.VMEM((groups - 1, 3, z_rows, cols), dtype),
-            pltpu.VMEM((2, groups + 1, 3, z_rows, cols), dtype),
-            pltpu.VMEM((2, z_rows, cols), dtype),
-            pltpu.VMEM((2, 2, z_rows, cols), dtype),
+            pltpu.VMEM((2, 2, groups, rows, cols), dtype),
+            pltpu.VMEM((groups, rows, cols), dtype),
+            pltpu.VMEM((2, groups, rows, cols), dtype),
+            pltpu.VMEM((2, rows, cols), dtype),
+            pltpu.VMEM((2, 2, 3, rows, cols), dtype),
+            pltpu.VMEM((2, rows, cols), dtype),
+            pltpu.VMEM((2, 2, rows, cols), dtype),
             pltpu.VMEM((bonds, half, cols), dtype),
             dma((4,)),
             dma((2,)),
@@ -554,11 +560,12 @@
             dma((groups // 2,)),
             dma((1,)),
             dma((2, groups, PIECES)),
+            dma((2, groups)),
+            dma((2, 2, groups)),
+            dma((1,)),
+            dma((2, groups)),
             dma((2,)),
-            dma((2, 2, groups)),
-            dma((2,)),
-            dma((2, groups - 1, PIECES)),
-            dma((2, groups - 1)),
+            dma((2, 2, 3)),
             dma((2,)),
             dma((2, 2)),
             dma((2,)),
@@ -581,6 +588,9 @@
         right_sizes,
         channel_shift,
     )
+    first, second = pl.pallas_call(hand_over, out_shape=(out, out), name="hand_over")(
+        first, second
+    )
     shape = (sectors, block_rows, cols)
     return first.reshape(shape), second.reshape(shape)
 

time: 111 us -> 110 us (level)
  local copies, waits for them, and re-layouts: 3.14 us -> 0 us
  Pallas kernels: 107 us -> 109 us
    unnamed x2 -> x0, local copies, waits for them, and re-layouts: 3.14 us -> none
    pallas_call x0 -> x1, Pallas kernels: none -> 1.68 us  [local(): pl.pallas_call(hand_over, out_shape=(out, out), name='hand_over')]
where the time goes in v2:
time: 110 us
  Pallas kernels  109 us (99%)
    pallas_call x1, Pallas kernels, local(): pl.pallas_call(kernel, out_shape=(out, out), in_specs=[pl.BlockSpec(memor...  107 us

profile of v2, /device:TPU:1, one launch (start us, length us, event | category | flops | bytes accessed | tf_op | source)
XLA Modules:
  0.0 109.7 jit_solution(10132293350481406043)
XLA Ops:
  0.6 107.4 %two_steps.1 = (bf16[16,2,16,128]{3,2,1,0:T(8,128)(2,1)}, bf16[16,2,16,128]{3,2,1,0:T(8,128)(2,1)}) custom-call(bf16[16,32,1024]{2,1,0:T(8,128)(2,1)} %wave.1, bf16[3,512,1024]{2,1,0:T(8,128)(2,1)} %bitcast.4, bf16[3,32,16,1024]{3,2,1,0:T(8,128)(2,1)} %bitcast.5, s32[16]{0:T(128)} %left_sizes.1, s32[16]{0:T(128)} %right_sizes.1, s32[24]{0:T(128)} %channel_shift.1), custom_call_target="tpu_custom_call" | custom-call | flops 12884901888 | bytes 9437184 | tf_op jit(solution)/shard_map/two_steps/pallas_call | solution.py:531
  108.0 1.7 %hand_over.1 = (bf16[16,2,16,128]{3,2,1,0:T(8,128)(2,1)}, bf16[16,2,16,128]{3,2,1,0:T(8,128)(2,1)}) custom-call(bf16[16,2,16,128]{3,2,1,0:T(8,128)(2,1)} %get-tuple-element.6.first, bf16[16,2,16,128]{3,2,1,0:T(8,128)(2,1)} %get-tuple-element.7.second), custom_call_target="tpu_custom_call" | custom-call | tf_op jit(solution)/shard_map/hand_over/pallas_call | solution.py:591

commit v3 on v2

--- a/solution.py
+++ b/solution.py
@@ -129,6 +129,9 @@
 
     swap_right.start()
 
+    def peer(i):
+        return (me + jnp.where(i <= sectors, sectors - 1 + i, bonds - i)) % bonds
+
     def piece_of_wave(p, chunk):
         return wave.at[
             p // 2,
@@ -140,7 +143,7 @@
     theirs = [1 - z % 2 + 2 * j for j in range(hops)]
 
     def scatter(j, i):
-        p = (me + i) % bonds
+        p = peer(i)
         remote(
             piece_of_wave(p, ours[j]),
             start_in.at[j, me],
@@ -228,6 +231,120 @@
                 block, block, ring_send.at[0], side_recv.at[j], (me, (z + way + groups) % groups)
             )
 
+        def images(d, pair):
+            blocks = [
+                right[order[d], pl.ds(chunk * per_chunk, per_chunk)].reshape(cols, -1)
+                for chunk in pair
+            ]
+            both = lax.dot_general(
+                mixed[d],
+                jnp.concatenate(blocks, axis=0),
+                (((1,), (1,)), ((), ())),
+                preferred_element_type=jnp.float32,
+            )
+            return both[:, :cols], both[:, cols:]
+
+        has_target = [(q < sectors - 1), (q > 0)]
+        has_source = [(q > 0), (q < sectors - 1)]
+
+        def to_sector(d, o, device=partner):
+            chunk = chunk_at(o)
+            return remote(
+                moved_out.at[d, chunk],
+                moved_in.at[step, d, chunk],
+                moved_send.at[d, o + hops - 1],
+                moved_recv.at[step, d, o + hops - 1],
+                device,
+            )
+
+        def late(d, device=partner):
+            return remote(
+                late_out.at[d], late_in.at[step, d], late_send.at[d], late_recv.at[step, d], device
+            )
+
+        def neighbour(d):
+            return (me + (2 if d == 0 else -2), z)
+
+        def to_beside(o, i):
+            side = (1 - o) // 2
+            source = moved_out.at[i, chunk_at(o)] if i < 2 else near_out.at[side]
+            return remote(
+                source,
+                beside_in.at[step, side, i],
+                beside_send.at[i // 2],
+                beside_recv.at[step, side, i],
+                (me, chunk_at(o)),
+            )
+
+        def partial(o):
+            slot = o + hops - 1
+            return remote(
+                part_out.at[slot],
+                part_in.at[step, slot],
+                part_send.at[0],
+                part_recv.at[step, slot],
+                (me, chunk_at(o - parent(o))),
+            )
+
+        def add_children(o, total):
+            for c in children(o):
+                partial(c).wait_recv()
+                total += part_in[step, c + hops - 1].astype(jnp.float32)
+            return total
+
+        def hop(o):
+            chunk = chunk_at(o)
+            total = near[chunk]
+            for d in range(2):
+
+                @pl.when(has_source[d])
+                def _():
+                    to_sector(d, o).wait_recv()
+
+                total += moved_in[step, d, chunk].astype(jnp.float32)
+            part_out[o + hops - 1] = add_children(o, total).astype(part_out.dtype)
+            partial(o).start()
+
+        def moved_pair(d, pair, offs):
+            blocks = images(d, pair)
+            for n, chunk in enumerate(pair):
+                moved_out[d, chunk] = blocks[n].astype(moved_out.dtype)
+            for u, some in offs:
+                for o in some:
+                    if o > REACH or hops == 2 and o == 2:
+
+                        @pl.when(u & has_target[d])
+                        def _():
+                            to_sector(d, o, neighbour(d)).start()
+
+                    if abs(o) == 1:
+
+                        @pl.when(u)
+                        def _():
+                            to_beside(o, d).start()
+
+        def near_pair(pair):
+            near[pair[0]], near[pair[1]] = images(2, pair)
+
+        def close(queue):
+            pair = [chunk_at(o) for o in pairs[0]]
+            for d in range(2):
+                run(queue, 1)
+                moved_pair(d, pair, [(True, pairs[0])])
+            run(queue, 1)
+            near_pair(pair)
+
+        def image_pair(u, inner):
+            first, second = pairs[-1]
+            for t in range(1, len(pairs) - 1):
+                first = jnp.where(u == t, pairs[t][0], first)
+                second = jnp.where(u == t, pairs[t][1], second)
+            pair = (chunk_at(first), chunk_at(second))
+            for d in range(2):
+                moved_pair(d, pair, [(u == t, pairs[t]) for t in range(1, len(pairs))])
+            near_pair(pair)
+            return inner
+
         @pl.when(step == 0)
         def _():
             def begin(j):
@@ -260,12 +377,13 @@
                 run(queue, 1 + j % 2)
                 if j % 2:
                     queue += mix_units(theirs[j - 1 : j + 1])
-            run(queue, len(queue))
+            run(queue, len(queue) - channels)
+            load_right.wait()
+            swap_right.wait()
+            close(queue)
             sent = start_in.at[:, pl.ds(0, bonds - 1)]
             await_sent(sent, scatter_send.at[0])
             await_sent(full.at[0, pl.ds(0, hops), :, 0], ring_send.at[0])
-            load_right.wait()
-            swap_right.wait()
 
         @pl.when(step == 1)
         def _():
@@ -291,112 +409,10 @@
                     run(queue, 2 - piece)
                 run(queue)
                 queue = mix_units([from_behind, from_ahead] if s < hops else [from_behind])
-            run(queue)
+            close(queue)
             await_sent(full.at[1, pl.ds(0, groups - 1), :, 0], ring_send.at[0])
 
-        def images(d, pair):
-            blocks = [
-                right[order[d], pl.ds(chunk * per_chunk, per_chunk)].reshape(cols, -1)
-                for chunk in pair
-            ]
-            both = lax.dot_general(
-                mixed[d],
-                jnp.concatenate(blocks, axis=0),
-                (((1,), (1,)), ((), ())),
-                preferred_element_type=jnp.float32,
-            )
-            return both[:, :cols], both[:, cols:]
-
-        has_target = [(q < sectors - 1), (q > 0)]
-        has_source = [(q > 0), (q < sectors - 1)]
-
-        def to_sector(d, o, device=partner):
-            chunk = chunk_at(o)
-            return remote(
-                moved_out.at[d, chunk],
-                moved_in.at[step, d, chunk],
-                moved_send.at[d, o + hops - 1],
-                moved_recv.at[step, d, o + hops - 1],
-                device,
-            )
-
-        def late(d, device=partner):
-            return remote(
-                late_out.at[d], late_in.at[step, d], late_send.at[d], late_recv.at[step, d], device
-            )
-
-        def neighbour(d):
-            return (me + (2 if d == 0 else -2), z)
-
-        def to_beside(o, i):
-            side = (1 - o) // 2
-            source = moved_out.at[i, chunk_at(o)] if i < 2 else near_out.at[side]
-            return remote(
-                source,
-                beside_in.at[step, side, i],
-                beside_send.at[i // 2],
-                beside_recv.at[step, side, i],
-                (me, chunk_at(o)),
-            )
-
-        def partial(o):
-            slot = o + hops - 1
-            return remote(
-                part_out.at[slot],
-                part_in.at[step, slot],
-                part_send.at[0],
-                part_recv.at[step, slot],
-                (me, chunk_at(o - parent(o))),
-            )
-
-        def add_children(o, total):
-            for c in children(o):
-                partial(c).wait_recv()
-                total += part_in[step, c + hops - 1].astype(jnp.float32)
-            return total
-
-        def hop(o):
-            chunk = chunk_at(o)
-            total = near[chunk]
-            for d in range(2):
-
-                @pl.when(has_source[d])
-                def _():
-                    to_sector(d, o).wait_recv()
-
-                total += moved_in[step, d, chunk].astype(jnp.float32)
-            part_out[o + hops - 1] = add_children(o, total).astype(part_out.dtype)
-            partial(o).start()
-
-        def image_pair(u, inner):
-            first, second = pairs[-1]
-            for t in range(len(pairs) - 1):
-                first = jnp.where(u == t, pairs[t][0], first)
-                second = jnp.where(u == t, pairs[t][1], second)
-            pair = (chunk_at(first), chunk_at(second))
-            for d in range(2):
-                blocks = images(d, pair)
-                for n, chunk in enumerate(pair):
-                    moved_out[d, chunk] = blocks[n].astype(moved_out.dtype)
-                for t, some in enumerate(pairs):
-                    for o in some:
-
-                        if o > REACH or hops == 2 and o == 2:
-
-                            @pl.when((u == t) & has_target[d])
-                            def _():
-                                to_sector(d, o, neighbour(d)).start()
-
-                        if abs(o) == 1:
-
-                            @pl.when((u == t))
-                            def _():
-                                to_beside(o, d).start()
-
-            near[pair[0]], near[pair[1]] = images(2, pair)
-            return inner
-
-        lax.fori_loop(0, len(pairs), image_pair, 0)
+        lax.fori_loop(1, len(pairs), image_pair, 0)
 
         @pl.when(step == 1)
         def _():
@@ -440,14 +456,14 @@
             send_after(-2, -3)
             hop(-3)
             merge_own()
-            send_after(0, 2)
+            send_after(0, -2)
             hop(2)
             hop(-2)
             for d in range(2):
 
                 @pl.when(has_target[d])
                 def _():
-                    to_sector(d, -2).wait_send()
+                    to_sector(d, 2).wait_send()
 
         total = near[z]
         for o in (1, -1):
@@ -492,7 +508,7 @@
 
     def send_back(out, block, slot):
         def one(i, carry):
-            p = (me + i) % bonds
+            p = peer(i)
             remote(
                 block.at[p], out.at[q, h], back_send.at[slot], back_recv.at[slot], (p, z)
             ).start()

time: 110 us -> 111 us (level)
    pallas_call x1, Pallas kernels: 107 us -> 109 us  [local(): pl.pallas_call(kernel, out_shape=(out, out), in_specs=[pl.BlockSpec(memor...]
where the time goes in v3:
time: 111 us
  Pallas kernels  110 us (99%)
    pallas_call x1, Pallas kernels, local(): pl.pallas_call(kernel, out_shape=(out, out), in_specs=[pl.BlockSpec(memor...  109 us

profile of v3, /device:TPU:1, one launch (start us, length us, event | category | flops | bytes accessed | tf_op | source)
XLA Modules:
  0.0 111.1 jit_solution(13858036482003917163)
XLA Ops:
  0.6 108.8 %two_steps.1 = (bf16[16,2,16,128]{3,2,1,0:T(8,128)(2,1)}, bf16[16,2,16,128]{3,2,1,0:T(8,128)(2,1)}) custom-call(bf16[16,32,1024]{2,1,0:T(8,128)(2,1)} %wave.1, bf16[3,512,1024]{2,1,0:T(8,128)(2,1)} %bitcast.4, bf16[3,32,16,1024]{3,2,1,0:T(8,128)(2,1)} %bitcast.5, s32[16]{0:T(128)} %left_sizes.1, s32[16]{0:T(128)} %right_sizes.1, s32[24]{0:T(128)} %channel_shift.1), custom_call_target="tpu_custom_call" | custom-call | flops 12884901888 | bytes 9437184 | tf_op jit(solution)/shard_map/two_steps/pallas_call | solution.py:547
  109.4 1.7 %hand_over.1 = (bf16[16,2,16,128]{3,2,1,0:T(8,128)(2,1)}, bf16[16,2,16,128]{3,2,1,0:T(8,128)(2,1)}) custom-call(bf16[16,2,16,128]{3,2,1,0:T(8,128)(2,1)} %get-tuple-element.6.first, bf16[16,2,16,128]{3,2,1,0:T(8,128)(2,1)} %get-tuple-element.7.second), custom_call_target="tpu_custom_call" | custom-call | tf_op jit(solution)/shard_map/hand_over/pallas_call | solution.py:607

commit v4 on v1

--- a/solution.py
+++ b/solution.py
@@ -7,12 +7,12 @@
 
 MESH = pl.DeviceIdType.MESH
 PIECES = 2
-Z_PART = 8
-LAG = 1
+Z_PART = 4
+LAG = 2
 
 
 def z_first_rows(rows):
-    return rows * Z_PART // 32
+    return max(16, rows * Z_PART // 512 * 16)
 
 
 def kernel(
@@ -85,6 +85,15 @@
 
     ahead = (me, chunk_at(1))
     behind = (me, chunk_at(-1))
+    reach = max(1, hops // 2)
+
+    def parent(o):
+        return 0 if abs(o) <= reach else (reach if o > 0 else -reach)
+
+    offsets = range(1 - hops, hops + 1)
+
+    def children(o):
+        return [c for c in offsets if c and parent(c) == o]
 
     def remote(source, target, send, recv, device):
         return pltpu.make_async_remote_copy(
@@ -114,10 +123,13 @@
         )
         return carry
 
-    pl.semaphore_signal(barrier, inc=1, device_id=ahead, device_id_type=MESH)
-    pl.semaphore_signal(barrier, inc=1, device_id=behind, device_id_type=MESH)
+    for distance in range(1, reach + 1):
+        for way in (distance, -distance):
+            pl.semaphore_signal(
+                barrier, inc=1, device_id=(me, chunk_at(way)), device_id_type=MESH
+            )
     lax.fori_loop(1, bonds, greet, 0)
-    pl.semaphore_wait(barrier, bonds + 1)
+    pl.semaphore_wait(barrier, bonds - 1 + 2 * reach)
 
     swap_right.start()
 
@@ -160,10 +172,6 @@
             def _():
                 moved_in[step, d] = jnp.zeros(moved_in.shape[2:], moved_in.dtype)
                 late_in[step, d] = jnp.zeros(late_in.shape[2:], late_in.dtype)
-
-        for k in range(2):
-            y_part_in[step, k] = jnp.zeros(y_part_in.shape[2:], y_part_in.dtype)
-            z_part_in[step, k] = jnp.zeros(z_part_in.shape[2:], z_part_in.dtype)
 
     def live(first, count, chunk=z):
         row = lax.broadcasted_iota(jnp.int32, (count, cols), 0) + first
@@ -291,10 +299,6 @@
             run(queue)
             await_sent(full.at[1, pl.ds(0, groups - 1), :, 0], ring_send.at[0])
 
-        def order_of(k):
-            distance = hops - (k + 1) // 2
-            return chunk_at(distance * (1 - 2 * (k % 2)))
-
         def images(d, pair):
             blocks = [
                 right[order[d], pl.ds(chunk * per_chunk, per_chunk)].reshape(cols, -1)
@@ -328,28 +332,24 @@
         def neighbour(d):
             return (me + (2 if d == 0 else -2), z)
 
-        def way_of(k):
-            return (me, chunk_at(1 - 2 * (k % 2)))
-
-        def z_partial(k, device=partner):
+        def z_partial(o):
+            slot = o + hops - 1
             return remote(
-                z_part_out.at[k],
-                z_part_in.at[step, k + 2],
+                z_part_out.at[slot],
+                z_part_in.at[step, slot],
                 part_send.at[0],
-                z_part_recv.at[step, k],
-                device,
-            )
-
-        def y_part(piece):
-            return pl.ds(piece * (y_rows // PIECES), y_rows // PIECES)
-
-        def y_partial(k, piece, device=partner):
+                z_part_recv.at[step, slot],
+                (me, chunk_at(o - parent(o))),
+            )
+
+        def y_partial(o):
+            slot = o + hops - 1
             return remote(
-                y_part_out.at[k, y_part(piece)],
-                y_part_in.at[step, k + 2, y_part(piece)],
+                y_part_out.at[slot],
+                y_part_in.at[step, slot],
                 part_send.at[1],
-                y_part_recv.at[step, k, piece],
-                device,
+                y_part_recv.at[step, slot],
+                (me, chunk_at(o - parent(o))),
             )
 
         def z_terms(chunk):
@@ -373,36 +373,40 @@
                 def _():
                     to_sector(d, chunk, k).wait_recv()
 
-        def z_hop(k):
-            chunk = order_of(k)
-
-            @pl.when((k >= 2))
-            def _():
-                z_partial(k - 2).wait_recv()
-
-            for i, term in enumerate(z_terms(chunk)):
-                term += z_part_in[step, k, i].astype(jnp.float32)
-                z_part_out[k, i] = term.astype(z_part_out.dtype)
-            z_partial(k, way_of(k)).start()
-
-        def y_hop(k):
-            chunk = order_of(k)
-            await_moved(k, chunk)
-            for piece in range(PIECES):
-                part = y_part(piece)
-
-                @pl.when((k >= 2))
-                def _():
-                    y_partial(k - 2, piece).wait_recv()
-
-                total = y_terms(chunk, part) + y_part_in[step, k, part].astype(jnp.float32)
-                y_part_out[k, part] = total.astype(y_part_out.dtype)
-                y_partial(k, piece, way_of(k)).start()
-
-        def round_of_ring(t, inner):
-            @pl.when(t < hops)
-            def _():
-                pair = (order_of(2 * t), order_of(2 * t + 1))
+        def z_sum(o):
+            terms = z_terms(chunk_at(o))
+            for c in children(o):
+                z_partial(c).wait_recv()
+                for i in range(3):
+                    terms[i] += z_part_in[step, c + hops - 1, i].astype(jnp.float32)
+            return terms
+
+        def z_hop(o):
+            for i, term in enumerate(z_sum(o)):
+                z_part_out[o + hops - 1, i] = term.astype(z_part_out.dtype)
+            z_partial(o).start()
+
+        def y_sum(o, k):
+            await_moved(k, chunk_at(o))
+            total = y_terms(chunk_at(o))
+            for c in children(o):
+                y_partial(c).wait_recv()
+                total += y_part_in[step, c + hops - 1].astype(jnp.float32)
+            return total
+
+        def y_hop(o, k):
+            y_part_out[o + hops - 1] = y_sum(o, k).astype(y_part_out.dtype)
+            y_partial(o).start()
+
+        pairs = [(hops if t == 0 else t - hops, hops - 1 - t) for t in range(hops)]
+
+        def round_of_tree(u, inner):
+            @pl.when(u < hops)
+            def _():
+                pair = (
+                    chunk_at(jnp.where(u == 0, hops, u - hops)),
+                    chunk_at(hops - 1 - u),
+                )
                 for d in range(2):
                     blocks = images(d, pair)
                     for n, chunk in enumerate(pair):
@@ -410,42 +414,47 @@
 
                         @pl.when(has_target[d])
                         def _():
-                            to_sector(d, chunk, 2 * t + n, neighbour(d)).start()
+                            to_sector(d, chunk, 2 * u + n, neighbour(d)).start()
 
                 near[pair[0]], near[pair[1]] = images(2, pair)
 
-            for hop, lag in ((z_hop, 1), (y_hop, LAG)):
-
-                @pl.when((t >= lag) & (t < lag + hops))
+            for t in range(hops):
+
+                @pl.when(u == t)
                 def _():
-                    hop(2 * (t - lag))
-
-                @pl.when((t >= lag) & (t < lag + hops - 1))
+                    for o in pairs[t]:
+                        if o and not children(o):
+                            z_hop(o)
+
+            @pl.when(u == hops - 1)
+            def _():
+                for o in offsets:
+                    if o and children(o):
+                        z_hop(o)
+
+            @pl.when(u == hops - 1 + LAG)
+            def _():
+                for i, term in enumerate(z_sum(0)):
+                    if i == 0:
+                        near[z, z_span] = term
+                    else:
+                        late_out[i - 1] = term.astype(late_out.dtype)
+
+                        @pl.when(has_target[i - 1])
+                        def _():
+                            late(i - 1, neighbour(i - 1)).start()
+
+            for t in range(hops):
+
+                @pl.when(u == t + LAG)
                 def _():
-                    hop(2 * (t - lag) + 1)
+                    for n, o in enumerate(pairs[t]):
+                        if o:
+                            y_hop(o, 2 * t + n)
 
             return inner
 
-        lax.fori_loop(0, hops + LAG, round_of_ring, 0)
-
-        z_total = z_terms(z)
-        for k in (groups - 3, groups - 2):
-            z_partial(k).wait_recv()
-            for i in range(3):
-                z_total[i] += z_part_in[step, k + 2, i].astype(jnp.float32)
-        for d in range(2):
-            late_out[d] = z_total[1 + d].astype(late_out.dtype)
-
-            @pl.when(has_target[d])
-            def _():
-                late(d, neighbour(d)).start()
-
-        await_moved(groups - 1, z)
-        total = y_terms(z)
-        for k in (groups - 3, groups - 2):
-            for piece in range(PIECES):
-                y_partial(k, piece).wait_recv()
-            total += y_part_in[step, k + 2].astype(jnp.float32)
+        lax.fori_loop(0, hops + LAG, round_of_tree, 0)
 
         def conclude(value, first, count):
             value = jnp.where(live(first, count), value, 0.0)
@@ -461,7 +470,7 @@
                 begin = full[0, z, span, h].reshape(count, cols).astype(jnp.float32)
                 last[span] = (2.0 * value - begin).astype(last.dtype).reshape(shape)
 
-        conclude(total, 0, y_rows)
+        conclude(y_sum(0, groups - 1), 0, y_rows)
         for d in range(2):
 
             @pl.when(has_source[d])
@@ -469,7 +478,7 @@
                 late(d).wait_recv()
 
         total = (
-            z_total[0]
+            near[z, z_span]
             + late_in[step, 0].astype(jnp.float32)
             + late_in[step, 1].astype(jnp.float32)
         )
@@ -482,8 +491,8 @@
                 await_sent(moved_out.at[d, :, y_span], moved_send.at[d])
                 late(d).wait_send()
 
-        await_sent(z_part_out, part_send.at[0])
-        await_sent(y_part_out, part_send.at[1])
+        await_sent(z_part_out.at[pl.ds(0, groups - 1)], part_send.at[0])
+        await_sent(y_part_out.at[pl.ds(0, groups - 1)], part_send.at[1])
         await_sent(full.at[step, :, :, 0], cross_send.at[0])
         return carry
 
@@ -507,6 +516,11 @@
     send_back(second_out, last, 1)
     finish(first_out, full.at[1, z, :, h], 0)
     finish(second_out, last, 1)
+
+
+def hand_over(first, second, first_out, second_out):
+    first_out[...] = first[...]
+    second_out[...] = second[...]
 
 
 def local(wavefunction, left_env, right_env, left_sizes, right_sizes, channel_shift):
@@ -537,10 +551,10 @@
             pltpu.VMEM((groups, rows, cols), jnp.float32),
             pltpu.VMEM((2, groups, rows, cols), dtype),
             pltpu.VMEM((2, 2, groups, y_rows, cols), dtype),
-            pltpu.VMEM((groups - 1, y_rows, cols), dtype),
-            pltpu.VMEM((2, groups + 1, y_rows, cols), dtype),
-            pltpu.VMEM((groups - 1, 3, z_rows, cols), dtype),
-            pltpu.VMEM((2, groups + 1, 3, z_rows, cols), dtype),
+            pltpu.VMEM((groups, y_rows, cols), dtype),
+            pltpu.VMEM((2, groups, y_rows, cols), dtype),
+            pltpu.VMEM((groups, 3, z_rows, cols), dtype),
+            pltpu.VMEM((2, groups, 3, z_rows, cols), dtype),
             pltpu.VMEM((2, z_rows, cols), dtype),
             pltpu.VMEM((2, 2, z_rows, cols), dtype),
             pltpu.VMEM((bonds, half, cols), dtype),
@@ -557,8 +571,8 @@
             dma((2,)),
             dma((2, 2, groups)),
             dma((2,)),
-            dma((2, groups - 1, PIECES)),
-            dma((2, groups - 1)),
+            dma((2, groups)),
+            dma((2, groups)),
             dma((2,)),
             dma((2, 2)),
             dma((2,)),
@@ -581,6 +595,9 @@
         right_sizes,
         channel_shift,
     )
+    first, second = pl.pallas_call(hand_over, out_shape=(out, out), name="hand_over")(
+        first, second
+    )
     shape = (sectors, block_rows, cols)
     return first.reshape(shape), second.reshape(shape)
 

time: 111 us -> 110 us (level)
  local copies, waits for them, and re-layouts: 3.14 us -> 0 us
  Pallas kernels: 107 us -> 109 us
    unnamed x2 -> x0, local copies, waits for them, and re-layouts: 3.14 us -> none
    pallas_call x0 -> x1, Pallas kernels: none -> 1.68 us  [local(): pl.pallas_call(hand_over, out_shape=(out, out), name='hand_over')]
where the time goes in v4:
time: 110 us
  Pallas kernels  109 us (99%)
    pallas_call x1, Pallas kernels, local(): pl.pallas_call(kernel, out_shape=(out, out), in_specs=[pl.BlockSpec(memor...  107 us

profile of v4, /device:TPU:1, one launch (start us, length us, event | category | flops | bytes accessed | tf_op | source)
XLA Modules:
  0.0 109.5 jit_solution(16996521771789521825)
XLA Ops:
  0.6 107.2 %two_steps.1 = (bf16[16,2,16,128]{3,2,1,0:T(8,128)(2,1)}, bf16[16,2,16,128]{3,2,1,0:T(8,128)(2,1)}) custom-call(bf16[16,32,1024]{2,1,0:T(8,128)(2,1)} %wave.1, bf16[3,512,1024]{2,1,0:T(8,128)(2,1)} %bitcast.4, bf16[3,32,16,1024]{3,2,1,0:T(8,128)(2,1)} %bitcast.5, s32[16]{0:T(128)} %left_sizes.1, s32[16]{0:T(128)} %right_sizes.1, s32[24]{0:T(128)} %channel_shift.1), custom_call_target="tpu_custom_call" | custom-call | flops 12884901888 | bytes 9437184 | tf_op jit(solution)/shard_map/two_steps/pallas_call | solution.py:539
  107.8 1.7 %hand_over.1 = (bf16[16,2,16,128]{3,2,1,0:T(8,128)(2,1)}, bf16[16,2,16,128]{3,2,1,0:T(8,128)(2,1)}) custom-call(bf16[16,2,16,128]{3,2,1,0:T(8,128)(2,1)} %get-tuple-element.6.first, bf16[16,2,16,128]{3,2,1,0:T(8,128)(2,1)} %get-tuple-element.7.second), custom_call_target="tpu_custom_call" | custom-call | tf_op jit(solution)/shard_map/hand_over/pallas_call | solution.py:598

commit v5 on v4

--- a/solution.py
+++ b/solution.py
@@ -9,6 +9,7 @@
 PIECES = 2
 Z_PART = 4
 LAG = 2
+SPLIT = 2
 
 
 def z_first_rows(rows):
@@ -304,12 +305,18 @@
                 right[order[d], pl.ds(chunk * per_chunk, per_chunk)].reshape(cols, -1)
                 for chunk in pair
             ]
-            both = lax.dot_general(
-                mixed[d],
-                jnp.concatenate(blocks, axis=0),
-                (((1,), (1,)), ((), ())),
-                preferred_element_type=jnp.float32,
-            )
+            block = jnp.concatenate(blocks, axis=0)
+            share_rows = rows // SPLIT
+            both = [
+                lax.dot_general(
+                    mixed[d, n * share_rows : (n + 1) * share_rows],
+                    block,
+                    (((1,), (1,)), ((), ())),
+                    preferred_element_type=jnp.float32,
+                )
+                for n in range(SPLIT)
+            ]
+            both = jnp.concatenate(both, axis=0)
             return both[:, :cols], both[:, cols:]
 
         has_target = [(q < sectors - 1), (q > 0)]

time: 110 us -> 108 us (0.982)
  Pallas kernels: 109 us -> 107 us
    pallas_call x1, Pallas kernels: 107 us -> 105 us  [local(): pl.pallas_call(kernel, out_shape=(out, out), in_specs=[pl.BlockSpec(memor...]
where the time goes in v5:
time: 108 us; the launch traced here: 107 us
  Pallas kernels  107 us (99%)
    pallas_call x1, Pallas kernels, local(): pl.pallas_call(kernel, out_shape=(out, out), in_specs=[pl.BlockSpec(memor...  105 us

profile of v5, /device:TPU:1, one launch (start us, length us, event | category | flops | bytes accessed | tf_op | source)
XLA Modules:
  0.0 107.4 jit_solution(10577607609359356424)
XLA Ops:
  0.6 105.1 %two_steps.1 = (bf16[16,2,16,128]{3,2,1,0:T(8,128)(2,1)}, bf16[16,2,16,128]{3,2,1,0:T(8,128)(2,1)}) custom-call(bf16[16,32,1024]{2,1,0:T(8,128)(2,1)} %wave.1, bf16[3,512,1024]{2,1,0:T(8,128)(2,1)} %bitcast.4, bf16[3,32,16,1024]{3,2,1,0:T(8,128)(2,1)} %bitcast.5, s32[16]{0:T(128)} %left_sizes.1, s32[16]{0:T(128)} %right_sizes.1, s32[24]{0:T(128)} %channel_shift.1), custom_call_target="tpu_custom_call" | custom-call | flops 12884901888 | bytes 9437184 | tf_op jit(solution)/shard_map/two_steps/pallas_call | solution.py:546
  105.7 1.7 %hand_over.1 = (bf16[16,2,16,128]{3,2,1,0:T(8,128)(2,1)}, bf16[16,2,16,128]{3,2,1,0:T(8,128)(2,1)}) custom-call(bf16[16,2,16,128]{3,2,1,0:T(8,128)(2,1)} %get-tuple-element.6.first, bf16[16,2,16,128]{3,2,1,0:T(8,128)(2,1)} %get-tuple-element.7.second), custom_call_target="tpu_custom_call" | custom-call | tf_op jit(solution)/shard_map/hand_over/pallas_call | solution.py:605
